TPU v7x, 32 devices: a whole 2x2x4 slice. The times are simulated.
32 devices in a mesh: wide: 16 (over z, y, core), narrow: 2 (over x).
Axes of the slice: x: 2, y: 2, z: 4, core: 2. Of those that a mesh axis runs over, the one named last changes fastest.
Arguments:
- right_side: float32 [96, 128, 256], P(('wide', 'narrow')), may hold values from -6 to 6
- diag_inverse: float32 [96, 128, 128], P(('wide', 'narrow')), may hold values from -1 to 1, as said below
- off_tiles: float32 [96, 48, 128, 128], P('wide', 'narrow'), may hold values from -0.078125 to 0.078125
- tile_columns: int32 [96, 48], P('wide', 'narrow'), may hold values from 0 to 95, as said below
- colors: int32 [96], replicated, may hold values from 0 to 2, as said below
Outputs:
- potentials: float32 [96, 128, 256], P(('wide', 'narrow'))
Inputs may be any that keep to these rules, and one draw needn't show every extreme that they name: `colors`: each device along wide+narrow owns 3 consecutive blocks, exactly 1 of each color. `tile_columns`: slot k of a block row names a block owned by a device whose narrow index is k // 24, and of another color than the row's block. `diag_inverse`: symmetric tiles.
All inputs are finite; a program needn't handle non-finite values.
Results may differ from a plain program's by a relative error of at most 0.0001.
Values sent between devices are 32-bit elements; how exact they have to be, the bound alone decides.
A program may use at most 128 MiB of HBM per device.

v0:
```python
from functools import partial
import jax
import jax.numpy as jnp
from jax import lax
from jax.sharding import PartitionSpec as P


def block_terms(stack, tile_rows, column_slots, column_hues, start, count):
    picked = stack[column_hues, column_slots]
    return jnp.einsum("rkab,rkbl->ral", tile_rows, picked, precision=lax.Precision.HIGHEST)


def sweep(source, sorted_inv, sorted_tiles, slot_of, color_of, wide_size, narrow_size, per_color):
    label_width = source.shape[2]
    tile_size = source.shape[1]
    copies = jnp.zeros((3, wide_size * per_color, tile_size, label_width), jnp.float32)
    pieces = [None, None, None]
    for section, color_now in enumerate((0, 1, 2, 1, 0)):
        offset = color_now * per_color
        local_side = source[offset : offset + per_color]
        if section > 0:
            row_low = color_now * narrow_size * per_color
            row_high = row_low + narrow_size * per_color
            term_fn = partial(
                block_terms,
                copies,
                sorted_tiles[row_low:row_high],
                slot_of[row_low:row_high],
                color_of[row_low:row_high],
            )
            summed = lax.psum_scatter(
                term_fn(jnp.int32(0), lax.axis_size("narrow") * per_color),
                "narrow",
                scatter_dimension=0,
                tiled=True,
            )
            local_side = local_side - summed
        updated = jnp.einsum(
            "rab,rbl->ral",
            sorted_inv[offset : offset + per_color],
            local_side,
            precision=lax.Precision.HIGHEST,
        )
        pieces[color_now] = updated
        if section < 4:
            gathered = lax.all_gather(updated, "wide", axis=0, tiled=True)
            copies = copies.at[color_now].set(gathered)
    return jnp.concatenate(pieces, axis=0)


def shards(right_side, diag_inverse, off_tiles, tile_columns, colors):
    wide_size = lax.axis_size("wide")
    narrow_size = lax.axis_size("narrow")
    wide_at = lax.axis_index("wide")
    narrow_at = lax.axis_index("narrow")
    row_count = off_tiles.shape[0]
    own_count = right_side.shape[0]
    per_color = own_count // 3
    block_total = colors.shape[0]
    row_colors = lax.dynamic_slice_in_dim(colors, wide_at * row_count, row_count)
    row_order = jnp.argsort(row_colors, stable=True)
    sorted_tiles = off_tiles[row_order]
    sorted_cols = tile_columns[row_order]
    owner_colors = colors.reshape(block_total // own_count, own_count)
    owner_order = jnp.argsort(owner_colors, axis=1, stable=True)
    owner_inverse = jnp.argsort(owner_order, axis=1)
    ranks = (owner_inverse - owner_colors * per_color).reshape(block_total)
    block_ids = jnp.arange(block_total, dtype=jnp.int32)
    slot_all = block_ids // (narrow_size * own_count) * per_color + ranks
    slot_of = slot_all[sorted_cols]
    color_of = colors[sorted_cols]
    own_start = (wide_at * narrow_size + narrow_at) * own_count
    own_colors = lax.dynamic_slice_in_dim(colors, own_start, own_count)
    own_order = jnp.argsort(own_colors, stable=True)
    own_inverse = jnp.argsort(own_order)
    sorted_inv = diag_inverse[own_order]
    sorted_side = right_side[own_order]
    result = sweep(
        sorted_side, sorted_inv, sorted_tiles, slot_of, color_of, wide_size, narrow_size, per_color
    )
    return result[own_inverse]


def solution(mesh):
    return jax.shard_map(
        shards,
        mesh=mesh,
        in_specs=(
            P(("wide", "narrow"), None, None),
            P(("wide", "narrow"), None, None),
            P("wide", "narrow", None, None),
            P("wide", "narrow"),
            P(),
        ),
        out_specs=P(("wide", "narrow"), None, None),
        check_vma=False,
    )
```

profile of v0, /device:TPU:0, one launch (start us, length us, event | category | flops | bytes accessed | tf_op | source)
XLA Modules:
  0.0 317.8 jit_solution(14142655278700782819)
XLA Ops:
  16.6 1.9 gather_fusion.4
  20.5 8.6 %gather_fusion.2 = f32[6,24,128,128]{3,2,1,0:T(8,128)} fusion(f32[6,24,128,128]{3,2,1,0:T(8,128)} %param.15, s32[1024]{0:T(1024)S(1)} %pad_clamp_fusion.2), kind=kCustom, calls=%fused_computation.2 | custom fusion | bytes 18874392 | tf_op jit(solution)/shard_map/gather | solution.py:62
  29.1 26.3 %all-gather.9.cloned.1.call-done = f32[2048,256]{1,0:T(8,128)} async-done(((f32[128,256]{1,0:T(8,128)}), f32[2048,256]{1,0:T(8,128)}) %all-gather.9.cloned.1.call-update) | async-done | bytes 2097168 | tf_op jit(solution)/shard_map/all_gather | solution.py:46
  55.4 5.1 %scatter.14 = f32[3,16,128,256]{3,2,1,0:T(8,128)} pad(f32[1,16,128,256]{3,2,1,0:T(8,128)} %bitcast.69, f32[]{:T(128)} %constant.133.clone.1), padding=0_2x0_0x0_0x0_0 | pad | bytes 8388612 | tf_op jit(solution)/shard_map/scatter | solution.py:47
  60.4 6.5 %gather_fusion.6 = f32[48,128,256]{2,1,0:T(8,128)} fusion(f32[3,16,128,256]{3,2,1,0:T(8,128)} %scatter.14, s32[48]{0:T(128)S(1)} %reshape.253), kind=kCustom, calls=%fused_computation.6 | custom fusion | bytes 12583296 | tf_op jit(solution)/shard_map/gather | solution.py:9
  66.9 9.7 %convolution_bitcast_fusion.3 = f32[2,128,256]{2,1,0:T(8,128)} fusion(f32[6,24,128,128]{3,2,1,0:T(8,128)} %gather_fusion.2, f32[2,24,128,256]{3,2,1,0:T(8,128)} %bitcast.65), kind=kOutput, calls=%fused_computation.14 | convolution fusion | flops 2415919104 | bytes 15990784 | tf_op jit(solution)/shard_map/rkab,rkbl->ral/dot_general | solution.py:10
  76.7 10.5 %reduce-scatter.5.cloned.1.call-done = f32[1,128,256]{2,1,0:T(8,128)} async-done(((f32[2,128,256]{2,1,0:T(8,128)}), f32[1,128,256]{2,1,0:T(8,128)}) %reduce-scatter.5.cloned.1.call-update) | async-done | bytes 131088 | tf_op jit(solution)/shard_map/reduce_scatter | solution.py:31
  87.3 1.8 fusion.6
  89.4 41.7 %all-gather.11.cloned.1.call-done = f32[2048,256]{1,0:T(8,128)} async-done(((f32[128,256]{1,0:T(8,128)}), f32[2048,256]{1,0:T(8,128)}) %all-gather.11.cloned.1.call-update) | async-done | bytes 2097168 | tf_op jit(solution)/shard_map/all_gather | solution.py:46
  131.1 3.2 %constant_dynamic-update-slice_fusion.2 = f32[3,16,128,256]{3,2,1,0:T(8,128)} fusion(f32[3,16,128,256]{3,2,1,0:T(8,128)} %scatter.14, f32[1,16,128,256]{3,2,1,0:T(8,128)} %bitcast.67), kind=kLoop, calls=%fused_computation.72 | loop fusion | bytes 4194304 | tf_op jit(solution)/shard_map/scatter | solution.py:47
  134.3 6.5 %gather_fusion.7 = f32[48,128,256]{2,1,0:T(8,128)} fusion(f32[3,16,128,256]{3,2,1,0:T(8,128)} %constant_dynamic-update-slice_fusion.2, s32[48]{0:T(128)S(1)} %reshape.259), kind=kCustom, calls=%fused_computation.7 | custom fusion | bytes 12583296 | tf_op jit(solution)/shard_map/gather | solution.py:9
  140.8 9.7 %convolution_bitcast_fusion.2 = f32[2,128,256]{2,1,0:T(8,128)} fusion(f32[6,24,128,128]{3,2,1,0:T(8,128)} %gather_fusion.2, f32[2,24,128,256]{3,2,1,0:T(8,128)} %bitcast.63), kind=kOutput, calls=%fused_computation.13 | convolution fusion | flops 2415919104 | bytes 15990784 | tf_op jit(solution)/shard_map/rkab,rkbl->ral/dot_general | solution.py:10
  150.6 10.5 %reduce-scatter.7.cloned.1.call-done = f32[1,128,256]{2,1,0:T(8,128)} async-done(((f32[2,128,256]{2,1,0:T(8,128)}), f32[1,128,256]{2,1,0:T(8,128)}) %reduce-scatter.7.cloned.1.call-update) | async-done | bytes 131088 | tf_op jit(solution)/shard_map/reduce_scatter | solution.py:31
  163.2 41.4 %all-gather.13.cloned.1.call-done = f32[2048,256]{1,0:T(8,128)} async-done(((f32[128,256]{1,0:T(8,128)}), f32[2048,256]{1,0:T(8,128)}) %all-gather.13.cloned.1.call-update) | async-done | bytes 2097168 | tf_op jit(solution)/shard_map/all_gather | solution.py:46
  204.6 3.1 constant_dynamic-update-slice_fusion.1
  207.7 6.5 %gather_fusion.8 = f32[48,128,256]{2,1,0:T(8,128)} fusion(f32[3,16,128,256]{3,2,1,0:T(8,128)} %constant_dynamic-update-slice_fusion.1, s32[48]{0:T(128)S(1)} %reshape.253), kind=kCustom, calls=%fused_computation.8 | custom fusion | bytes 12583296 | tf_op jit(solution)/shard_map/gather | solution.py:9
  214.2 9.7 %convolution_bitcast_fusion.1 = f32[2,128,256]{2,1,0:T(8,128)} fusion(f32[6,24,128,128]{3,2,1,0:T(8,128)} %gather_fusion.2, f32[2,24,128,256]{3,2,1,0:T(8,128)} %bitcast.64), kind=kOutput, calls=%fused_computation.12 | convolution fusion | flops 2415919104 | bytes 15990784 | tf_op jit(solution)/shard_map/rkab,rkbl->ral/dot_general | solution.py:10
  224.0 10.5 %reduce-scatter.9.cloned.1.call-done = f32[1,128,256]{2,1,0:T(8,128)} async-done(((f32[2,128,256]{2,1,0:T(8,128)}), f32[1,128,256]{2,1,0:T(8,128)}) %reduce-scatter.9.cloned.1.call-update) | async-done | bytes 131088 | tf_op jit(solution)/shard_map/reduce_scatter | solution.py:31
  234.5 1.8 fusion.4
  236.7 41.7 %all-gather.15.cloned.1.call-done = f32[2048,256]{1,0:T(8,128)} async-done(((f32[128,256]{1,0:T(8,128)}), f32[2048,256]{1,0:T(8,128)}) %all-gather.15.cloned.1.call-update) | async-done | bytes 2097168 | tf_op jit(solution)/shard_map/all_gather | solution.py:46
  278.4 3.2 %constant_dynamic-update-slice_fusion = f32[3,16,128,256]{3,2,1,0:T(8,128)} fusion(f32[3,16,128,256]{3,2,1,0:T(8,128)} %constant_dynamic-update-slice_fusion.1, f32[1,16,128,256]{3,2,1,0:T(8,128)} %bitcast.66), kind=kLoop, calls=%fused_computation.70 | loop fusion | bytes 4194304 | tf_op jit(solution)/shard_map/scatter | solution.py:47
  281.6 6.5 %gather_fusion.9 = f32[48,128,256]{2,1,0:T(8,128)} fusion(f32[3,16,128,256]{3,2,1,0:T(8,128)} %constant_dynamic-update-slice_fusion, s32[48]{0:T(128)S(1)} %reshape.271), kind=kCustom, calls=%fused_computation.9 | custom fusion | bytes 12583296 | tf_op jit(solution)/shard_map/gather | solution.py:9
  288.1 9.8 %convolution_bitcast_fusion = f32[2,128,256]{2,1,0:T(8,128)} fusion(f32[6,24,128,128]{3,2,1,0:T(8,128)} %gather_fusion.2, f32[2,24,128,256]{3,2,1,0:T(8,128)} %bitcast.62), kind=kOutput, calls=%fused_computation.11 | convolution fusion | flops 2415919104 | bytes 15990784 | tf_op jit(solution)/shard_map/rkab,rkbl->ral/dot_general | solution.py:10
  298.6 9.8 %reduce-scatter.11.cloned.1.call-done = f32[1,128,256]{2,1,0:T(8,128)} async-done(((f32[2,128,256]{2,1,0:T(8,128)}), f32[1,128,256]{2,1,0:T(8,128)}) %reduce-scatter.11.cloned.1.call-update) | async-done | bytes 131088 | tf_op jit(solution)/shard_map/reduce_scatter | solution.py:31
  (72 shorter events, 18.1 us)
Async XLA Ops:
  6.5 1.6 copy-start
  6.5 48.8 %all-gather.9.cloned.1.call-start = ((), (), s32[]{:S(2)}) async-start(), calls=%async_computation.8 | async-start | bytes 2228224 | tf_op jit(solution)/shard_map/all_gather | solution.py:46
  11.1 76.2 %reduce-scatter.5.cloned.1.call-start = ((), (), s32[]{:S(2)}) async-start(), calls=%async_computation.4 | async-start | bytes 393216 | tf_op jit(solution)/shard_map/reduce_scatter | solution.py:31
  76.7 54.4 %all-gather.11.cloned.1.call-start = ((), (), s32[]{:S(2)}) async-start(), calls=%async_computation.9 | async-start | bytes 2228224 | tf_op jit(solution)/shard_map/all_gather | solution.py:46
  89.1 72.1 %reduce-scatter.7.cloned.1.call-start = ((), (), s32[]{:S(2)}) async-start(), calls=%async_computation.5 | async-start | bytes 393216 | tf_op jit(solution)/shard_map/reduce_scatter | solution.py:31
  150.6 54.0 %all-gather.13.cloned.1.call-start = ((), (), s32[]{:S(2)}) async-start(), calls=%async_computation.10 | async-start | bytes 2228224 | tf_op jit(solution)/shard_map/all_gather | solution.py:46
  163.0 71.5 %reduce-scatter.9.cloned.1.call-start = ((), (), s32[]{:S(2)}) async-start(), calls=%async_computation.6 | async-start | bytes 393216 | tf_op jit(solution)/shard_map/reduce_scatter | solution.py:31
  223.9 54.4 %all-gather.15.cloned.1.call-start = ((), (), s32[]{:S(2)}) async-start(), calls=%async_computation.11 | async-start | bytes 2228224 | tf_op jit(solution)/shard_map/all_gather | solution.py:46
  236.4 72.1 %reduce-scatter.11.cloned.1.call-start = ((), (), s32[]{:S(2)}) async-start(), calls=%async_computation.7 | async-start | bytes 393216 | tf_op jit(solution)/shard_map/reduce_scatter | solution.py:31
  288.1 21.6 %copy-start.1 = (f32[128,256]{1,0:T(8,128)S(1)}, f32[128,256]{1,0:T(8,128)}, u32[]{:S(2)}) copy-start(f32[128,256]{1,0:T(8,128)} %fusion.1) | copy-start | bytes 393220
  288.1 21.6 %copy-start.2 = (f32[128,256]{1,0:T(8,128)S(1)}, f32[128,256]{1,0:T(8,128)}, u32[]{:S(2)}) copy-start(f32[128,256]{1,0:T(8,128)} %fusion.4) | copy-start | bytes 393220
Sparse Core Ops, SparseCore 0:
  11.2 44.0 all-gather.8
  76.8 10.4 reduce-scatter.4
  89.7 41.4 all-gather.10
  150.7 10.4 reduce-scatter.6
  163.2 41.3 all-gather.12
  224.1 10.4 reduce-scatter.8
  236.9 41.4 all-gather.14
  298.0 10.4 reduce-scatter.10
where the time goes:
time: 318 us
  waiting for transfers between devices  193 us (61%)
  local copies, waits for them, and re-layouts  60.7 us (19%)
  matrix products  46.6 us (15%)
  between operations  13.6 us (4%)
  other arithmetic  3.94 us (1%)
    all_gather x4, waiting for transfers between devices, sweep(): gathered = lax.all_gather(updated, 'wide', axis=0, tiled=True)  151 us
    reduce_scatter x4, waiting for transfers between devices, sweep(): lax.psum_scatter(term_fn(jnp.int32(0), lax.axis_size('narrow') * per_colo...  41.4 us
    dot_general x4, matrix products, block_terms(): jnp.einsum('rkab,rkbl->ral', tile_rows, picked, precision=lax.Precision.H...  39 us
    gather x4, local copies, waits for them, and re-layouts, block_terms(): picked = stack[column_hues, column_slots]  26 us
    scatter x4, local copies, waits for them, and re-layouts, sweep(): copies = copies.at[color_now].set(gathered)  14.5 us
    gather x1, local copies, waits for them, and re-layouts, shards(): sorted_tiles = off_tiles[row_order]  8.58 us
    dot_general x5, matrix products, sweep(): jnp.einsum('rab,rbl->ral', sorted_inv[offset:offset + per_color], local_s...  7.55 us
  transfers between devices with their start and end apart: 8, of which 8 were waited for; matrix products, arithmetic and copies ran while one was open for 6% of the time, Pallas kernels for 0%

commit v1 on v0

--- a/solution.py
+++ b/solution.py
@@ -43,7 +43,16 @@
         )
         pieces[color_now] = updated
         if section < 4:
-            gathered = lax.all_gather(updated, "wide", axis=0, tiled=True)
+            ring = [updated]
+            for hop in range(15):
+                ring.append(
+                    lax.ppermute(ring[-1], "wide", [(dev, (dev + 1) % 16) for dev in range(16)])
+                )
+            gathered = jnp.roll(
+                jnp.concatenate(ring[::-1], axis=0),
+                (lax.axis_index("wide") + 1) * ring[0].shape[0],
+                axis=0,
+            )
             copies = copies.at[color_now].set(gathered)
     return jnp.concatenate(pieces, axis=0)
 

time: 318 us -> 568 us (1.79)
  waiting for transfers between devices: 193 us -> 449 us
  local copies, waits for them, and re-layouts: 60.7 us -> 50 us
  other arithmetic: 3.94 us -> 9.7 us
    ppermute x0 -> x60, waiting for transfers between devices: none -> 412 us  [sweep(): lax.ppermute(ring[-1], 'wide', [(dev, (dev + 1) % 16) for dev in range(16)])]
    all_gather x4 -> x0, waiting for transfers between devices: 151 us -> none  [sweep(): gathered = lax.all_gather(updated, 'wide', axis=0, tiled=True)]
    scatter x4 -> x1, local copies, waits for them, and re-layouts: 14.5 us -> 3.36 us  [sweep(): copies = copies.at[color_now].set(gathered)]
  transfers between devices with their start and end apart: 8 -> 64, of which waited for: 8 -> 63; matrix products, arithmetic and copies ran while one was open for 6% -> 3% of each run, Pallas kernels for 0% -> 0%
where the time goes in v1:
time: 568 us; the launch traced here: 567 us
  waiting for transfers between devices  449 us (79%)
  local copies, waits for them, and re-layouts  50 us (9%)
  matrix products  43.9 us (8%)
  between operations  13.9 us (2%)
  other arithmetic  9.7 us (2%)
    ppermute x60, waiting for transfers between devices, sweep(): lax.ppermute(ring[-1], 'wide', [(dev, (dev + 1) % 16) for dev in range(16)])  412 us
    dot_general x4, matrix products, block_terms(): jnp.einsum('rkab,rkbl->ral', tile_rows, picked, precision=lax.Precision.H...  39 us
    reduce_scatter x4, waiting for transfers between devices, sweep(): lax.psum_scatter(term_fn(jnp.int32(0), lax.axis_size('narrow') * per_colo...  36.2 us
    gather x4, local copies, waits for them, and re-layouts, block_terms(): picked = stack[column_hues, column_slots]  26.1 us
  transfers between devices with their start and end apart: 64, of which 63 were waited for; matrix products, arithmetic and copies ran while one was open for 3% of the time, Pallas kernels for 0%

profile of v1, /device:TPU:0, one launch (start us, length us, event | category | flops | bytes accessed | tf_op | source)
XLA Modules:
  0.0 567.0 jit_solution(9997540870178803604)
XLA Ops:
  14.0 7.6 %collective-permute-done = f32[1,128,256]{2,1,0:T(8,128)S(1)} collective-permute-done((f32[1,128,256]{2,1,0:T(8,128)S(1)}, f32[1,128,256]{2,1,0:T(8,128)S(1)}, u32[]{:S(2)}, u32[]{:S(2)}) %collective-permute-start) | collective-permute-done | bytes 131104 | tf_op jit(solution)/shard_map/ppermute | solution.py:49
  21.6 7.1 %collective-permute-done.1 = f32[1,128,256]{2,1,0:T(8,128)S(1)} collective-permute-done((f32[1,128,256]{2,1,0:T(8,128)S(1)}, f32[1,128,256]{2,1,0:T(8,128)S(1)}, u32[]{:S(2)}, u32[]{:S(2)}) %collective-permute-start.1) | collective-permute-done | bytes 131104 | tf_op jit(solution)/shard_map/ppermute | solution.py:49
  28.7 7.1 %collective-permute-done.2 = f32[1,128,256]{2,1,0:T(8,128)S(1)} collective-permute-done((f32[1,128,256]{2,1,0:T(8,128)S(1)}, f32[1,128,256]{2,1,0:T(8,128)S(1)}, u32[]{:S(2)}, u32[]{:S(2)}) %collective-permute-start.2) | collective-permute-done | bytes 131104 | tf_op jit(solution)/shard_map/ppermute | solution.py:49
  35.8 7.1 %collective-permute-done.3 = f32[1,128,256]{2,1,0:T(8,128)S(1)} collective-permute-done((f32[1,128,256]{2,1,0:T(8,128)S(1)}, f32[1,128,256]{2,1,0:T(8,128)S(1)}, u32[]{:S(2)}, u32[]{:S(2)}) %collective-permute-start.3) | collective-permute-done | bytes 131104 | tf_op jit(solution)/shard_map/ppermute | solution.py:49
  42.9 7.1 %collective-permute-done.4 = f32[1,128,256]{2,1,0:T(8,128)S(1)} collective-permute-done((f32[1,128,256]{2,1,0:T(8,128)S(1)}, f32[1,128,256]{2,1,0:T(8,128)S(1)}, u32[]{:S(2)}, u32[]{:S(2)}) %collective-permute-start.4) | collective-permute-done | bytes 131104 | tf_op jit(solution)/shard_map/ppermute | solution.py:49
  50.0 7.1 %collective-permute-done.5 = f32[1,128,256]{2,1,0:T(8,128)S(1)} collective-permute-done((f32[1,128,256]{2,1,0:T(8,128)S(1)}, f32[1,128,256]{2,1,0:T(8,128)S(1)}, u32[]{:S(2)}, u32[]{:S(2)}) %collective-permute-start.5) | collective-permute-done | bytes 131104 | tf_op jit(solution)/shard_map/ppermute | solution.py:49
  57.1 7.1 %collective-permute-done.6 = f32[1,128,256]{2,1,0:T(8,128)S(1)} collective-permute-done((f32[1,128,256]{2,1,0:T(8,128)S(1)}, f32[1,128,256]{2,1,0:T(8,128)S(1)}, u32[]{:S(2)}, u32[]{:S(2)}) %collective-permute-start.6) | collective-permute-done | bytes 131104 | tf_op jit(solution)/shard_map/ppermute | solution.py:49
  64.2 7.1 %collective-permute-done.7 = f32[1,128,256]{2,1,0:T(8,128)S(1)} collective-permute-done((f32[1,128,256]{2,1,0:T(8,128)S(1)}, f32[1,128,256]{2,1,0:T(8,128)S(1)}, u32[]{:S(2)}, u32[]{:S(2)}) %collective-permute-start.7) | collective-permute-done | bytes 131104 | tf_op jit(solution)/shard_map/ppermute | solution.py:49
  71.3 7.1 %collective-permute-done.8 = f32[1,128,256]{2,1,0:T(8,128)S(1)} collective-permute-done((f32[1,128,256]{2,1,0:T(8,128)S(1)}, f32[1,128,256]{2,1,0:T(8,128)S(1)}, u32[]{:S(2)}, u32[]{:S(2)}) %collective-permute-start.8) | collective-permute-done | bytes 131104 | tf_op jit(solution)/shard_map/ppermute | solution.py:49
  78.4 7.1 %collective-permute-done.9 = f32[1,128,256]{2,1,0:T(8,128)S(1)} collective-permute-done((f32[1,128,256]{2,1,0:T(8,128)S(1)}, f32[1,128,256]{2,1,0:T(8,128)S(1)}, u32[]{:S(2)}, u32[]{:S(2)}) %collective-permute-start.9) | collective-permute-done | bytes 131104 | tf_op jit(solution)/shard_map/ppermute | solution.py:49
  113.9 8.5 %gather_fusion.2 = f32[6,24,128,128]{3,2,1,0:T(8,128)} fusion(f32[6,24,128,128]{3,2,1,0:T(8,128)} %param.17, s32[1024]{0:T(1024)S(1)} %pad_clamp_fusion.2), kind=kCustom, calls=%fused_computation.2 | custom fusion | bytes 18874392 | tf_op jit(solution)/shard_map/gather | solution.py:71
  133.1 9.7 %convolution_bitcast_fusion.3 = f32[2,128,256]{2,1,0:T(8,128)} fusion(f32[6,24,128,128]{3,2,1,0:T(8,128)} %gather_fusion.2, f32[2,24,128,256]{3,2,1,0:T(8,128)} %bitcast.81), kind=kOutput, calls=%fused_computation.33 | convolution fusion | flops 2415919104 | bytes 15990784 | tf_op jit(solution)/shard_map/rkab,rkbl->ral/dot_general | solution.py:10
  142.9 13.4 %reduce-scatter.5.cloned.1.call-done = f32[1,128,256]{2,1,0:T(8,128)} async-done(((f32[2,128,256]{2,1,0:T(8,128)}), f32[1,128,256]{2,1,0:T(8,128)}) %reduce-scatter.5.cloned.1.call-update) | async-done | bytes 131088 | tf_op jit(solution)/shard_map/reduce_scatter | solution.py:31
  164.6 7.1 %collective-permute-done.16 = f32[1,128,256]{2,1,0:T(8,128)S(1)} collective-permute-done((f32[1,128,256]{2,1,0:T(8,128)S(1)}, f32[1,128,256]{2,1,0:T(8,128)S(1)}, u32[]{:S(2)}, u32[]{:S(2)}) %collective-permute-start.16) | collective-permute-done | bytes 131104 | tf_op jit(solution)/shard_map/ppermute | solution.py:49
  171.7 7.1 %collective-permute-done.17 = f32[1,128,256]{2,1,0:T(8,128)S(1)} collective-permute-done((f32[1,128,256]{2,1,0:T(8,128)S(1)}, f32[1,128,256]{2,1,0:T(8,128)S(1)}, u32[]{:S(2)}, u32[]{:S(2)}) %collective-permute-start.17) | collective-permute-done | bytes 131104 | tf_op jit(solution)/shard_map/ppermute | solution.py:49
  272.6 9.7 %convolution_bitcast_fusion.2 = f32[2,128,256]{2,1,0:T(8,128)} fusion(f32[6,24,128,128]{3,2,1,0:T(8,128)} %gather_fusion.2, f32[2,24,128,256]{3,2,1,0:T(8,128)} %bitcast.79), kind=kOutput, calls=%fused_computation.32 | convolution fusion | flops 2415919104 | bytes 15990784 | tf_op jit(solution)/shard_map/rkab,rkbl->ral/dot_general | solution.py:10
  282.4 7.8 %reduce-scatter.7.cloned.1.call-done = f32[1,128,256]{2,1,0:T(8,128)} async-done(((f32[2,128,256]{2,1,0:T(8,128)}), f32[1,128,256]{2,1,0:T(8,128)}) %reduce-scatter.7.cloned.1.call-update) | async-done | bytes 131088 | tf_op jit(solution)/shard_map/reduce_scatter | solution.py:31
  348.2 7.1 %collective-permute-done.38 = f32[1,128,256]{2,1,0:T(8,128)S(1)} collective-permute-done((f32[1,128,256]{2,1,0:T(8,128)S(1)}, f32[1,128,256]{2,1,0:T(8,128)S(1)}, u32[]{:S(2)}, u32[]{:S(2)}) %collective-permute-start.38) | collective-permute-done | bytes 131104 | tf_op jit(solution)/shard_map/ppermute | solution.py:49
  369.4 7.1 %collective-permute-done.41 = f32[1,128,256]{2,1,0:T(8,128)S(1)} collective-permute-done((f32[1,128,256]{2,1,0:T(8,128)S(1)}, f32[1,128,256]{2,1,0:T(8,128)S(1)}, u32[]{:S(2)}, u32[]{:S(2)}) %collective-permute-start.41) | collective-permute-done | bytes 131104 | tf_op jit(solution)/shard_map/ppermute | solution.py:49
  406.4 9.7 %convolution_bitcast_fusion.1 = f32[2,128,256]{2,1,0:T(8,128)} fusion(f32[6,24,128,128]{3,2,1,0:T(8,128)} %gather_fusion.2, f32[2,24,128,256]{3,2,1,0:T(8,128)} %bitcast.80), kind=kOutput, calls=%fused_computation.31 | convolution fusion | flops 2415919104 | bytes 15990784 | tf_op jit(solution)/shard_map/rkab,rkbl->ral/dot_general | solution.py:10
  416.2 7.9 %reduce-scatter.9.cloned.1.call-done = f32[1,128,256]{2,1,0:T(8,128)} async-done(((f32[2,128,256]{2,1,0:T(8,128)}), f32[1,128,256]{2,1,0:T(8,128)}) %reduce-scatter.9.cloned.1.call-update) | async-done | bytes 131088 | tf_op jit(solution)/shard_map/reduce_scatter | solution.py:31
  439.5 7.1 %collective-permute-done.47 = f32[1,128,256]{2,1,0:T(8,128)S(1)} collective-permute-done((f32[1,128,256]{2,1,0:T(8,128)S(1)}, f32[1,128,256]{2,1,0:T(8,128)S(1)}, u32[]{:S(2)}, u32[]{:S(2)}) %collective-permute-start.47) | collective-permute-done | bytes 131104 | tf_op jit(solution)/shard_map/ppermute | solution.py:49
  460.7 7.1 %collective-permute-done.50 = f32[1,128,256]{2,1,0:T(8,128)S(1)} collective-permute-done((f32[1,128,256]{2,1,0:T(8,128)S(1)}, f32[1,128,256]{2,1,0:T(8,128)S(1)}, u32[]{:S(2)}, u32[]{:S(2)}) %collective-permute-start.50) | collective-permute-done | bytes 131104 | tf_op jit(solution)/shard_map/ppermute | solution.py:49
  540.3 9.8 %convolution_bitcast_fusion = f32[2,128,256]{2,1,0:T(8,128)} fusion(f32[6,24,128,128]{3,2,1,0:T(8,128)} %gather_fusion.2, f32[2,24,128,256]{3,2,1,0:T(8,128)} %bitcast.78), kind=kOutput, calls=%fused_computation.30 | convolution fusion | flops 2415919104 | bytes 15990784 | tf_op jit(solution)/shard_map/rkab,rkbl->ral/dot_general | solution.py:10
  (244 shorter events, 362.6 us)
Async XLA Ops:
  6.5 149.8 %reduce-scatter.5.cloned.1.call-start = ((), (), s32[]{:S(2)}) async-start(), calls=%async_computation.4 | async-start | bytes 393216 | tf_op jit(solution)/shard_map/reduce_scatter | solution.py:31
  13.5 8.1 %collective-permute-start = (f32[1,128,256]{2,1,0:T(8,128)S(1)}, f32[1,128,256]{2,1,0:T(8,128)S(1)}, u32[]{:S(2)}, u32[]{:S(2)}) collective-permute-start(f32[1,128,256]{2,1,0:T(8,128)S(1)} %convolution_bitcast_fusion.8), channel_id=1, source_target_pairs={{0,2},{2,4},{4,6},{6,8},{8,10},{10,12},{12,14},{14,16},{16,18},{18... | collective-permute-start | bytes 393224 | tf_op jit(solution)/shard_map/ppermute | solution.py:49
  21.6 7.1 %collective-permute-start.1 = (f32[1,128,256]{2,1,0:T(8,128)S(1)}, f32[1,128,256]{2,1,0:T(8,128)S(1)}, u32[]{:S(2)}, u32[]{:S(2)}) collective-permute-start(f32[1,128,256]{2,1,0:T(8,128)S(1)} %collective-permute-done), channel_id=1, source_target_pairs={{0,2},{2,4},{4,6},{6,8},{8,10},{10,12},{12,14},{14,16},{16,18},{18... | collective-permute-start | bytes 393224 | tf_op jit(solution)/shard_map/ppermute | solution.py:49
  28.7 7.1 %collective-permute-start.2 = (f32[1,128,256]{2,1,0:T(8,128)S(1)}, f32[1,128,256]{2,1,0:T(8,128)S(1)}, u32[]{:S(2)}, u32[]{:S(2)}) collective-permute-start(f32[1,128,256]{2,1,0:T(8,128)S(1)} %collective-permute-done.1), channel_id=1, source_target_pairs={{0,2},{2,4},{4,6},{6,8},{8,10},{10,12},{12,14},{14,16},{16,18},{18... | collective-permute-start | bytes 393224 | tf_op jit(solution)/shard_map/ppermute | solution.py:49
  35.8 7.1 %collective-permute-start.3 = (f32[1,128,256]{2,1,0:T(8,128)S(1)}, f32[1,128,256]{2,1,0:T(8,128)S(1)}, u32[]{:S(2)}, u32[]{:S(2)}) collective-permute-start(f32[1,128,256]{2,1,0:T(8,128)S(1)} %collective-permute-done.2), channel_id=1, source_target_pairs={{0,2},{2,4},{4,6},{6,8},{8,10},{10,12},{12,14},{14,16},{16,18},{18... | collective-permute-start | bytes 393224 | tf_op jit(solution)/shard_map/ppermute | solution.py:49
  42.9 7.1 %collective-permute-start.4 = (f32[1,128,256]{2,1,0:T(8,128)S(1)}, f32[1,128,256]{2,1,0:T(8,128)S(1)}, u32[]{:S(2)}, u32[]{:S(2)}) collective-permute-start(f32[1,128,256]{2,1,0:T(8,128)S(1)} %collective-permute-done.3), channel_id=1, source_target_pairs={{0,2},{2,4},{4,6},{6,8},{8,10},{10,12},{12,14},{14,16},{16,18},{18... | collective-permute-start | bytes 393224 | tf_op jit(solution)/shard_map/ppermute | solution.py:49
  50.0 7.1 %collective-permute-start.5 = (f32[1,128,256]{2,1,0:T(8,128)S(1)}, f32[1,128,256]{2,1,0:T(8,128)S(1)}, u32[]{:S(2)}, u32[]{:S(2)}) collective-permute-start(f32[1,128,256]{2,1,0:T(8,128)S(1)} %collective-permute-done.4), channel_id=1, source_target_pairs={{0,2},{2,4},{4,6},{6,8},{8,10},{10,12},{12,14},{14,16},{16,18},{18... | collective-permute-start | bytes 393224 | tf_op jit(solution)/shard_map/ppermute | solution.py:49
  57.1 7.1 %collective-permute-start.6 = (f32[1,128,256]{2,1,0:T(8,128)S(1)}, f32[1,128,256]{2,1,0:T(8,128)S(1)}, u32[]{:S(2)}, u32[]{:S(2)}) collective-permute-start(f32[1,128,256]{2,1,0:T(8,128)S(1)} %collective-permute-done.5), channel_id=1, source_target_pairs={{0,2},{2,4},{4,6},{6,8},{8,10},{10,12},{12,14},{14,16},{16,18},{18... | collective-permute-start | bytes 393224 | tf_op jit(solution)/shard_map/ppermute | solution.py:49
  64.2 7.1 %collective-permute-start.7 = (f32[1,128,256]{2,1,0:T(8,128)S(1)}, f32[1,128,256]{2,1,0:T(8,128)S(1)}, u32[]{:S(2)}, u32[]{:S(2)}) collective-permute-start(f32[1,128,256]{2,1,0:T(8,128)S(1)} %collective-permute-done.6), channel_id=1, source_target_pairs={{0,2},{2,4},{4,6},{6,8},{8,10},{10,12},{12,14},{14,16},{16,18},{18... | collective-permute-start | bytes 393224 | tf_op jit(solution)/shard_map/ppermute | solution.py:49
  71.3 7.1 %collective-permute-start.8 = (f32[1,128,256]{2,1,0:T(8,128)S(1)}, f32[1,128,256]{2,1,0:T(8,128)S(1)}, u32[]{:S(2)}, u32[]{:S(2)}) collective-permute-start(f32[1,128,256]{2,1,0:T(8,128)S(1)} %collective-permute-done.7), channel_id=1, source_target_pairs={{0,2},{2,4},{4,6},{6,8},{8,10},{10,12},{12,14},{14,16},{16,18},{18... | collective-permute-start | bytes 393224 | tf_op jit(solution)/shard_map/ppermute | solution.py:49
  78.4 7.1 %collective-permute-start.9 = (f32[1,128,256]{2,1,0:T(8,128)S(1)}, f32[1,128,256]{2,1,0:T(8,128)S(1)}, u32[]{:S(2)}, u32[]{:S(2)}) collective-permute-start(f32[1,128,256]{2,1,0:T(8,128)S(1)} %collective-permute-done.8), channel_id=1, source_target_pairs={{0,2},{2,4},{4,6},{6,8},{8,10},{10,12},{12,14},{14,16},{16,18},{18... | collective-permute-start | bytes 393224 | tf_op jit(solution)/shard_map/ppermute | solution.py:49
  85.5 7.1 %collective-permute-start.10 = (f32[1,128,256]{2,1,0:T(8,128)S(1)}, f32[1,128,256]{2,1,0:T(8,128)S(1)}, u32[]{:S(2)}, u32[]{:S(2)}) collective-permute-start(f32[1,128,256]{2,1,0:T(8,128)S(1)} %collective-permute-done.9), channel_id=1, source_target_pairs={{0,2},{2,4},{4,6},{6,8},{8,10},{10,12},{12,14},{14,16},{16,18},{18... | collective-permute-start | bytes 393224 | tf_op jit(solution)/shard_map/ppermute | solution.py:49
  92.6 7.1 %collective-permute-start.11 = (f32[1,128,256]{2,1,0:T(8,128)S(1)}, f32[1,128,256]{2,1,0:T(8,128)S(1)}, u32[]{:S(2)}, u32[]{:S(2)}) collective-permute-start(f32[1,128,256]{2,1,0:T(8,128)S(1)} %collective-permute-done.10), channel_id=1, source_target_pairs={{0,2},{2,4},{4,6},{6,8},{8,10},{10,12},{12,14},{14,16},{16,18},{18... | collective-permute-start | bytes 393224 | tf_op jit(solution)/shard_map/ppermute | solution.py:49
  99.6 7.1 %collective-permute-start.12 = (f32[1,128,256]{2,1,0:T(8,128)S(1)}, f32[1,128,256]{2,1,0:T(8,128)S(1)}, u32[]{:S(2)}, u32[]{:S(2)}) collective-permute-start(f32[1,128,256]{2,1,0:T(8,128)S(1)} %collective-permute-done.11), channel_id=1, source_target_pairs={{0,2},{2,4},{4,6},{6,8},{8,10},{10,12},{12,14},{14,16},{16,18},{18... | collective-permute-start | bytes 393224 | tf_op jit(solution)/shard_map/ppermute | solution.py:49
  106.7 7.1 %collective-permute-start.13 = (f32[1,128,256]{2,1,0:T(8,128)S(1)}, f32[1,128,256]{2,1,0:T(8,128)S(1)}, u32[]{:S(2)}, u32[]{:S(2)}) collective-permute-start(f32[1,128,256]{2,1,0:T(8,128)S(1)} %collective-permute-done.12), channel_id=1, source_target_pairs={{0,2},{2,4},{4,6},{6,8},{8,10},{10,12},{12,14},{14,16},{16,18},{18... | collective-permute-start | bytes 393224 | tf_op jit(solution)/shard_map/ppermute | solution.py:49
  113.8 8.6 %collective-permute-start.14 = (f32[1,128,256]{2,1,0:T(8,128)S(1)}, f32[1,128,256]{2,1,0:T(8,128)S(1)}, u32[]{:S(2)}, u32[]{:S(2)}) collective-permute-start(f32[1,128,256]{2,1,0:T(8,128)S(1)} %collective-permute-done.13), channel_id=1, source_target_pairs={{0,2},{2,4},{4,6},{6,8},{8,10},{10,12},{12,14},{14,16},{16,18},{18... | collective-permute-start | bytes 393224 | tf_op jit(solution)/shard_map/ppermute | solution.py:49
  142.9 147.3 %reduce-scatter.7.cloned.1.call-start = ((), (), s32[]{:S(2)}) async-start(), calls=%async_computation.5 | async-start | bytes 393216 | tf_op jit(solution)/shard_map/reduce_scatter | solution.py:31
  157.5 7.1 %collective-permute-start.15 = (f32[1,128,256]{2,1,0:T(8,128)S(1)}, f32[1,128,256]{2,1,0:T(8,128)S(1)}, u32[]{:S(2)}, u32[]{:S(2)}) collective-permute-start(f32[1,128,256]{2,1,0:T(8,128)S(1)} %convolution_bitcast_fusion.7), channel_id=1, source_target_pairs={{0,2},{2,4},{4,6},{6,8},{8,10},{10,12},{12,14},{14,16},{16,18},{18... | collective-permute-start | bytes 393224 | tf_op jit(solution)/shard_map/ppermute | solution.py:49
  256.8 7.1 %collective-permute-start.29 = (f32[1,128,256]{2,1,0:T(8,128)S(1)}, f32[1,128,256]{2,1,0:T(8,128)S(1)}, u32[]{:S(2)}, u32[]{:S(2)}) collective-permute-start(f32[1,128,256]{2,1,0:T(8,128)S(1)} %collective-permute-done.28), channel_id=1, source_target_pairs={{0,2},{2,4},{4,6},{6,8},{8,10},{10,12},{12,14},{14,16},{16,18},{18... | collective-permute-start | bytes 393224 | tf_op jit(solution)/shard_map/ppermute | solution.py:49
  282.3 141.7 %reduce-scatter.9.cloned.1.call-start = ((), (), s32[]{:S(2)}) async-start(), calls=%async_computation.6 | async-start | bytes 393216 | tf_op jit(solution)/shard_map/reduce_scatter | solution.py:31
  291.4 7.1 %collective-permute-start.30 = (f32[1,128,256]{2,1,0:T(8,128)S(1)}, f32[1,128,256]{2,1,0:T(8,128)S(1)}, u32[]{:S(2)}, u32[]{:S(2)}) collective-permute-start(f32[1,128,256]{2,1,0:T(8,128)S(1)} %convolution_bitcast_fusion.6), channel_id=1, source_target_pairs={{0,2},{2,4},{4,6},{6,8},{8,10},{10,12},{12,14},{14,16},{16,18},{18... | collective-permute-start | bytes 393224 | tf_op jit(solution)/shard_map/ppermute | solution.py:49
  416.1 141.9 %reduce-scatter.11.cloned.1.call-start = ((), (), s32[]{:S(2)}) async-start(), calls=%async_computation.7 | async-start | bytes 393216 | tf_op jit(solution)/shard_map/reduce_scatter | solution.py:31
  425.2 7.1 %collective-permute-start.45 = (f32[1,128,256]{2,1,0:T(8,128)S(1)}, f32[1,128,256]{2,1,0:T(8,128)S(1)}, u32[]{:S(2)}, u32[]{:S(2)}) collective-permute-start(f32[1,128,256]{2,1,0:T(8,128)S(1)} %convolution_bitcast_fusion.5), channel_id=1, source_target_pairs={{0,2},{2,4},{4,6},{6,8},{8,10},{10,12},{12,14},{14,16},{16,18},{18... | collective-permute-start | bytes 393224 | tf_op jit(solution)/shard_map/ppermute | solution.py:49
  489.1 7.1 %collective-permute-start.54 = (f32[1,128,256]{2,1,0:T(8,128)S(1)}, f32[1,128,256]{2,1,0:T(8,128)S(1)}, u32[]{:S(2)}, u32[]{:S(2)}) collective-permute-start(f32[1,128,256]{2,1,0:T(8,128)S(1)} %collective-permute-done.53), channel_id=1, source_target_pairs={{0,2},{2,4},{4,6},{6,8},{8,10},{10,12},{12,14},{14,16},{16,18},{18... | collective-permute-start | bytes 393224 | tf_op jit(solution)/shard_map/ppermute | solution.py:49
  (43 other events, 389.7 us)
Sparse Core Ops, SparseCore 0:
  143.0 13.2 reduce-scatter.4
  282.4 7.7 reduce-scatter.6
  416.2 7.7 reduce-scatter.8
  550.2 7.7 reduce-scatter.10
